TPU v7x, 32 devices: a whole 2x2x4 slice. The times are simulated.
32 devices in a mesh: freq: 8 (over y, x, core), blk: 4 (over z).
Axes of the slice: x: 2, y: 2, z: 4, core: 2. Of those that a mesh axis runs over, the one named last changes fastest.
Arguments:
- traces: bfloat16 [32, 4096, 1024], P(('blk', 'freq')), may hold values from -6 to 6
- fir: float32 [128], replicated, may hold values from -0.5 to 0.5
- targets: int32 [256], replicated, may hold values from 0 to 31
- band: int32 [2], replicated, may hold values from 1 to 512, as said below
Outputs:
- multiples: float32 [32, 2, 256, 4096], P('freq', None, None, 'blk')
Inputs may be any that keep to these rules, and one draw needn't show every extreme that they name: band[1] is 512 and band[1] - band[0] is at least 256.
All inputs are finite; a program needn't handle non-finite values.
Results may differ from a plain program's by a relative error of at most 0.019.
Values may be sent and summed in bfloat16 or wider, within the bound.
A program may use at most 128 MiB of HBM per device.

v0:
```python
import math

import jax
import jax.numpy as jnp
from jax import lax
from jax.sharding import PartitionSpec as P

FREQ_DEV = 4


def phase_table(band, freq_count, time_count):
    band_low = band[0]
    band_high = band[1]
    freq_index = jnp.arange(freq_count, dtype=jnp.int32)
    numerator = band_low * freq_count + (band_high - band_low) * freq_index
    time_index = jnp.arange(time_count, dtype=jnp.int32)
    turn_count = jnp.mod(time_index[:, None] * numerator[None, :], freq_count * time_count)
    phase_angle = turn_count.astype(jnp.float32) * (2.0 * math.pi / (freq_count * time_count))
    table = jnp.stack([jnp.cos(phase_angle), -jnp.sin(phase_angle)], axis=2) * (
        1.0 / math.sqrt(time_count)
    )
    return table.reshape(time_count, 2 * freq_count)


def split_parts(values):
    high_part = values.astype(jnp.bfloat16)
    low_part = (values - high_part.astype(jnp.float32)).astype(jnp.bfloat16)
    return (high_part, low_part)


def block_left(chosen):
    return jnp.stack(
        [
            jnp.concatenate([chosen[:, 0], -chosen[:, 1]], 1),
            jnp.concatenate([chosen[:, 1], chosen[:, 0]], 1),
        ],
        1,
    )


def column_products(chosen, columns, weight_scale):
    freq_dev, parts, shot_count, col_width = columns.shape
    right_block = columns.reshape(freq_dev, 2 * shot_count, col_width)
    summed = jnp.einsum(
        "fojk,fjr->fokr", block_left(chosen), right_block, preferred_element_type=jnp.float32
    )
    return summed * weight_scale


def local_targets(columns, targets, col_stride):
    picked = jnp.take(columns[..., ::col_stride], targets, axis=2)
    return jnp.swapaxes(picked, 2, 3)


def section_plan(spectrum, targets, col_stride, weight_scale):
    row_layout = lax.all_to_all(spectrum, "freq", split_axis=0, concat_axis=2, tiled=True)
    columns = lax.all_to_all(row_layout, "blk", split_axis=3, concat_axis=2, tiled=True)
    chosen = lax.all_gather(local_targets(columns, targets, col_stride), "blk", axis=2, tiled=True)
    return column_products(chosen, columns, weight_scale)


def per_device(traces, fir, targets, band):
    shot_dev, rec_count, time_count = traces.shape
    freq_devs = lax.axis_size("freq")
    blk_devs = lax.axis_size("blk")
    freq_count = FREQ_DEV * freq_devs
    shot_count = shot_dev * freq_devs * blk_devs
    col_stride = rec_count // shot_count
    tap_count = fir.shape[0]
    block_count = time_count // tap_count
    row_total = shot_dev * rec_count
    dft_table = phase_table(band, freq_count, time_count).reshape(
        block_count, tap_count, 2 * freq_count
    )
    tap_index = jnp.arange(tap_count, dtype=jnp.int32)
    lag_table = jnp.mod(tap_index[None, :] - tap_index[:, None], tap_count)
    circulant = jnp.sum(
        jnp.where(lag_table[:, :, None] == tap_index[None, None, :], fir[None, None, :], 0.0),
        axis=2,
    )
    lower_part = jnp.where(tap_index[None, :] >= tap_index[:, None], circulant, 0.0)
    upper_part = jnp.where(tap_index[None, :] < tap_index[:, None], circulant, 0.0)
    signal = traces.reshape(row_total, block_count, tap_count)
    lower_high, lower_low = split_parts(lower_part)
    upper_high, upper_low = split_parts(upper_part)
    earlier = signal[:, :-1]
    carried = jnp.einsum("rna,ab->rnb", earlier, upper_high, preferred_element_type=jnp.float32)
    carried = carried + jnp.einsum(
        "rna,ab->rnb", earlier, upper_low, preferred_element_type=jnp.float32
    )
    carried = jnp.concatenate([jnp.zeros((row_total, 1, tap_count), jnp.float32), carried], 1)
    shaped = jnp.einsum("rna,ab->rnb", signal, lower_high, preferred_element_type=jnp.float32)
    shaped = (
        shaped
        + jnp.einsum("rna,ab->rnb", signal, lower_low, preferred_element_type=jnp.float32)
        + carried
    )
    shaped_high, shaped_low = split_parts(shaped)
    table_high, table_low = split_parts(dft_table)
    spectrum = jnp.einsum(
        "rnb,nbc->cr", shaped_high, table_high, preferred_element_type=jnp.float32
    )
    spectrum = spectrum + jnp.einsum(
        "rnb,nbc->cr", shaped_high, table_low, preferred_element_type=jnp.float32
    )
    spectrum = spectrum + jnp.einsum(
        "rnb,nbc->cr", shaped_low, table_high, preferred_element_type=jnp.float32
    )
    spectrum = spectrum.astype(jnp.bfloat16).reshape(freq_count, 2, shot_dev, rec_count)
    weight_scale = 1.0 / math.sqrt(shot_count)
    return section_plan(spectrum, targets, col_stride, weight_scale)


def solution(mesh):
    placed = (P(("blk", "freq"), None, None), P(), P(), P())
    return jax.shard_map(
        per_device,
        mesh=mesh,
        in_specs=placed,
        out_specs=P("freq", None, None, "blk"),
        check_vma=False,
    )
```

profile of v0, /device:TPU:0, one launch (start us, length us, event | category | flops | bytes accessed | tf_op | source)
XLA Modules:
  0.0 191.2 jit_solution(4319317506778272300)
XLA Ops:
  0.0 0.0 copy-start.4
  0.0 11.9 %copy.90 = bf16[1,4096,1024]{1,2,0:T(8,128)(2,1)} copy(bf16[1,4096,1024]{2,1,0:T(8,128)(2,1)} %param.4) | data formatting | bytes 16777216 | tf_op args[0]
  12.0 0.0 copy-done.4
  12.0 5.1 %select_reduce_fusion = f32[128,128]{1,0:T(8,128)S(1)} fusion(f32[128]{0:T(128)S(1)} %copy-done.4, s32[128,128]{1,0:T(8,128)S(1)} %add_select_fusion.1), kind=kLoop, calls=%fused_computation.5 | loop fusion | flops 6275072 | bytes 131584 | tf_op jit(solution)/shard_map/reduce_sum | solution.py:77
  17.1 0.0 copy-start.1
  17.1 10.5 %fusion.1 = f32[128,4096,7]{1,0,2:T(8,128)} fusion(bf16[4096,8,128]{0,2,1:T(8,128)(2,1)} %bitcast.69, f32[128,128]{1,0:T(8,128)S(1)} %select_reduce_fusion), kind=kOutput, calls=%fused_computation.7 | convolution fusion | flops 939556864 | bytes 22085632 | tf_op jit(solution)/shard_map/rna,ab->rnb/dot_general | solution.py:87
  27.6 0.0 copy-done.1
  27.6 8.1 %fusion.29 = f32[128,4096,8]{1,0,2:T(8,128)} fusion(bf16[4096,8,128]{0,2,1:T(8,128)(2,1)S(1)} %bitcast.71, f32[128,128]{1,0:T(8,128)S(1)} %select_reduce_fusion), kind=kOutput, calls=%fused_computation.55 | convolution fusion | flops 1073774592 | bytes 25231360 | tf_op jit(solution)/shard_map/rna,ab->rnb/dot_general | solution.py:92
  35.7 0.0 copy-start.2
  35.7 9.4 %add_bitcast_fusion = f32[4096,7,128]{0,2,1:T(8,128)} fusion(f32[128,4096,7]{1,0,2:T(8,128)} %fusion.1, bf16[4096,8,128]{0,2,1:T(8,128)(2,1)S(1)} %bitcast.72, f32[128,128]{1,0:T(8,128)S(1)} %select_reduce_fusion), kind=kOutput, calls=%fused_computation.3 | convolution fusion | flops 943292416 | bytes 36765696 | tf_op jit(solution)/shard_map/rna,ab->rnb/dot_general | solution.py:88
  45.2 0.0 copy-done.2
  45.2 0.7 fusion.48
  47.8 0.6 fusion.20
  48.4 0.2 copy.88
  48.6 0.2 mul.84
  48.8 20.5 %bitcast_add_fusion = f32[4096,8,128]{0,2,1:T(8,128)} fusion(f32[4096,7,128]{0,2,1:T(8,128)} %add_bitcast_fusion, f32[128,4096,8]{1,0,2:T(8,128)} %fusion.29, bf16[4096,8,128]{0,2,1:T(8,128)(2,1)} %bitcast.70, f32[128,128]{1,0:T(8,128)S(1)} %select_reduce_fusion), kind=kOutput, calls=%fused_computation.1 | convolution fusion | flops 1082228736 | bytes 56688640 | tf_op jit(solution)/shard_map/rna,ab->rnb/dot_general | solution.py:95
  69.4 0.0 copy-start
  69.4 7.5 %convolution_bitcast_fusion.1 = f32[64,4096]{1,0:T(8,128)S(1)} fusion(f32[8,128,64]{1,0,2:T(8,128)S(1)} %mul.84, f32[4096,8,128]{0,2,1:T(8,128)} %bitcast_add_fusion), kind=kOutput, calls=%fused_computation.14 | convolution fusion | flops 541065216 | bytes 18087936 | tf_op jit(solution)/shard_map/rnb,nbc->cr/dot_general | solution.py:100
  76.9 3.1 %copy-done = f32[4096,8,128]{0,2,1:T(8,128)S(1)} copy-done((f32[4096,8,128]{0,2,1:T(8,128)S(1)}, f32[4096,8,128]{0,2,1:T(8,128)}, u32[]{:S(2)}) %copy-start) | copy-done | bytes 16777240
  79.9 1.6 fusion.4
  81.5 1.6 fusion.7
  83.1 0.3 reshape.151
  83.4 14.7 %all_to_all.36 = bf16[32,2,1,4096]{3,1,2,0:T(2,128)(2,1)S(1)} all-to-all(bf16[32,2,1,4096]{3,1,2,0:T(2,128)(2,1)S(1)} %bitcast.78), channel_id=1, replica_groups=mesh['freq'=8,'blk'=4] {'freq'}, dimensions={0} | all-to-all | bytes 1048576 | tf_op jit(solution)/shard_map/all_to_all | solution.py:56
  98.1 0.0 copy-start.3
  98.1 9.2 %copy.103 = bf16[4,2,8,4096]{2,0,1,3:T(4,128)(2,1)} copy(bf16[4,2,8,4096]{3,1,0,2:T(2,128)(2,1)S(1)} %bitcast.77) | data formatting | bytes 1048576 | tf_op jit(solution)/shard_map/all_to_all | solution.py:56
  107.4 11.3 %reshape.170 = bf16[4,2,32768]{2,1,0:T(2,128)(2,1)} reshape(bf16[4096,2,4,8]{3,2,1,0:T(4,128)(2,1)} %bitcast.75) | data formatting | bytes 1048576
  118.7 4.8 %all-to-all-start.1 = ((bf16[4,2,32768]{2,1,0:T(2,128)(2,1)}), bf16[4,2,32768]{2,1,0:T(2,128)(2,1)S(1)}, u32[]{:S(2)}, u32[]{:S(2)}) async-start(bf16[4,2,32768]{2,1,0:T(2,128)(2,1)} %reshape.170), calls=%async_computation.1 | async-start | bytes 1048576 | tf_op jit(solution)/shard_map/all_to_all | solution.py:57
  123.5 0.0 copy-done.3
  123.6 13.8 %all-to-all-done.1 = bf16[4,2,32768]{2,1,0:T(2,128)(2,1)S(1)} async-done(((bf16[4,2,32768]{2,1,0:T(2,128)(2,1)}), bf16[4,2,32768]{2,1,0:T(2,128)(2,1)S(1)}, u32[]{:S(2)}, u32[]{:S(2)}) %all-to-all-start.1) | async-done | bytes 524320 | tf_op jit(solution)/shard_map/all_to_all | solution.py:57
  137.4 11.0 %reshape.171 = bf16[4096,2,4,8]{3,2,1,0:T(4,128)(2,1)} reshape(bf16[4,2,32768]{2,1,0:T(2,128)(2,1)S(1)} %all-to-all-done.1) | data formatting | bytes 1048576
  148.4 11.7 %copy.105 = bf16[4,2,4,8,1024]{4,0,3,2,1:T(4,128)(2,1)S(1)} copy(bf16[4,2,4,8,1024]{3,0,1,4,2:T(4,128)(2,1)} %bitcast.73) | data formatting | bytes 1048576 | tf_op jit(solution)/shard_map/all_to_all | solution.py:57
  160.1 0.7 slice.23
  160.8 1.2 gather_fusion
  162.0 0.3 copy.106
  162.3 13.3 %all_gather.3 = bf16[4,2,32,256]{3,2,0,1:T(8,128)(2,1)S(1)} all-gather(bf16[4,2,8,256]{3,2,0,1:T(8,128)(2,1)S(1)} %select_bitcast_fusion), channel_id=1, replica_groups=mesh['freq'=8,'blk'=4] {'blk'}, dimensions={2}, use_global_device_ids=true | all-gather | bytes 163840 | tf_op jit(solution)/shard_map/all_gather | solution.py:58
  175.7 10.8 %copy.108 = bf16[4,2,4,8,1024]{4,3,2,1,0:T(8,128)(2,1)S(1)} copy(bf16[4,2,4,8,1024]{3,0,1,4,2:T(4,128)(2,1)} %bitcast.74) | data formatting | bytes 1048576 | tf_op jit(solution)/shard_map/all_to_all | solution.py:57
  186.5 4.7 %broadcast_multiply_fusion = f32[4,2,256,1024]{3,2,1,0:T(8,128)} fusion(bf16[4,64,1024,1]{2,1,3,0:T(8,128)(2,1)S(1)} %bitcast.76, bf16[4,1,64,256]{3,2,1,0:T(8,128)(2,1)S(1)} %get-tuple-element.8, bf16[4,1,64,256]{3,2,1,0:T(8,128)(2,1)S(1)} %get-tuple-element.7), kind=kOutput, calls=%fused_computation.16 | convolution fusion | flops 270663680 | bytes 9175040 | tf_op jit(solution)/shard_map/fojk,fjr->fokr/dot_general | solution.py:44
  (10 shorter events, 0.1 us)
Async XLA Ops:
  0.0 11.9 %copy-start.4 = (f32[128]{0:T(128)S(1)}, f32[128]{0:T(128)}, u32[]{:S(2)}) copy-start(f32[128]{0:T(128)} %param.5) | copy-start | bytes 1540
  17.1 10.5 %copy-start.1 = (bf16[1,4096,1024]{1,2,0:T(8,128)(2,1)S(1)}, bf16[1,4096,1024]{1,2,0:T(8,128)(2,1)}, u32[]{:S(2)}) copy-start(bf16[1,4096,1024]{1,2,0:T(8,128)(2,1)} %copy.90) | copy-start | bytes 25165828
  35.7 9.5 %copy-start.2 = (s32[2]{0:T(128)S(1)}, s32[2]{0:T(128)}, u32[]{:S(2)}) copy-start(s32[2]{0:T(128)} %param.7) | copy-start | bytes 28
  69.4 10.5 %copy-start = (f32[4096,8,128]{0,2,1:T(8,128)S(1)}, f32[4096,8,128]{0,2,1:T(8,128)}, u32[]{:S(2)}) copy-start(f32[4096,8,128]{0,2,1:T(8,128)} %bitcast_add_fusion) | copy-start | bytes 50331652
  98.1 25.4 %copy-start.3 = (s32[256]{0:T(256)S(1)}, s32[256]{0:T(256)}, u32[]{:S(2)}) copy-start(s32[256]{0:T(256)} %param.6) | copy-start | bytes 3076
  118.7 18.7 %all-to-all-start.1 = ((bf16[4,2,32768]{2,1,0:T(2,128)(2,1)}), bf16[4,2,32768]{2,1,0:T(2,128)(2,1)S(1)}, u32[]{:S(2)}, u32[]{:S(2)}) async-start(bf16[4,2,32768]{2,1,0:T(2,128)(2,1)} %reshape.170), calls=%async_computation.1 | async-start | bytes 1048576 | tf_op jit(solution)/shard_map/all_to_all | solution.py:57
where the time goes:
time: 192 us; the launch traced here: 191 us
  local copies, waits for them, and re-layouts  72.7 us (38%)
  matrix products  63.9 us (33%)
  blocking collectives  28.1 us (15%)
  waiting for transfers between devices  13.8 us (7%)
  other arithmetic  5.83 us (3%)
  starting transfers between devices  4.85 us (3%)
  between operations  2.08 us (1%)
    unnamed x13, local copies, waits for them, and re-layouts  37.3 us
    all_to_all x2, local copies, waits for them, and re-layouts, section_plan(): lax.all_to_all(row_layout, 'blk', split_axis=3, concat_axis=2, tiled=True)  22.5 us
    dot_general x1, matrix products, per_device(): jnp.einsum('rna,ab->rnb', signal, lower_low, preferred_element_type=jnp.f...  20.5 us
    all_to_all x1, blocking collectives, section_plan(): lax.all_to_all(spectrum, 'freq', split_axis=0, concat_axis=2, tiled=True)  14.7 us
    all_to_all x1, waiting for transfers between devices, section_plan(): lax.all_to_all(row_layout, 'blk', split_axis=3, concat_axis=2, tiled=True)  13.8 us
    all_gather x1, blocking collectives, section_plan(): lax.all_gather(local_targets(columns, targets, col_stride), 'blk', axis=2...  13.3 us
    dot_general x1, matrix products, per_device(): jnp.einsum('rna,ab->rnb', earlier, upper_high, preferred_element_type=jnp...  10.5 us
    dot_general x1, matrix products, per_device(): jnp.einsum('rna,ab->rnb', earlier, upper_low, preferred_element_type=jnp....  9.45 us
  transfers between devices with their start and end apart: 1, of which 1 were waited for; matrix products, arithmetic and copies ran while one was open for 0% of the time, Pallas kernels for 0%

commit v1 on v0

v1 whole, which is shorter than its diff:
```python
import functools
import math

import jax
import jax.numpy as jnp
from jax import lax
from jax.experimental import pallas as pl
from jax.experimental.pallas import tpu as pltpu
from jax.sharding import PartitionSpec as P

FREQ_DEV = 4
PARTS = 2 * FREQ_DEV
ROWS = 2 * PARTS
VMEM_LIMIT = 56 * 2**20
MESH = pl.DeviceIdType.MESH
NT_DIMS = (((1,), (1,)), ((), ()))


def dot(a, b, dims=(((1,), (0,)), ((), ())), precision=None):
    return lax.dot_general(a, b, dims, precision=precision, preferred_element_type=jnp.float32)


def cos_turns(turns):
    w = (0.25 - jnp.abs(turns - 0.5)) * (2.0 * math.pi)
    w2 = w * w
    total = jnp.full_like(w, 1.0 / math.factorial(13))
    for order in (11, 9, 7, 5, 3, 1):
        sign = 1.0 if order % 4 == 1 else -1.0
        total = total * w2 + sign / math.factorial(order)
    return -(total * w)


def send_kernel(
    freq_devs, blk_devs, col_stride,
    band_ref, fir_ref, traces_ref, recv_ref,
    traces_buf, spots_buf, table, outgoing, chunk_sem, spot_sem, own_sem, send_sem, recv_sem,
):
    me_f = lax.axis_index("freq")
    me_b = lax.axis_index("blk")
    me = me_b * freq_devs + me_f
    n = freq_devs * blk_devs
    spots, _, time_count = traces_buf.shape
    rec_count = spots * col_stride
    width = rec_count // blk_devs
    half = width // 2
    freq_count = FREQ_DEV * freq_devs
    cols = 2 * freq_count
    taps = fir_ref.shape[1]
    per = width // col_stride
    spot_lanes = outgoing.shape[3] - half

    def spot_copy():
        return pltpu.make_async_copy(
            traces_ref.at[:, pl.ds(0, 16), :], spots_buf, spot_sem
        )

    def chunk_copy(step):
        block = lax.rem(me_b + step + 1, blk_devs)
        return pltpu.make_async_copy(
            traces_ref.at[pl.ds(block * per, per)],
            traces_buf.at[pl.ds(step * per, per)],
            chunk_sem.at[step],
        )

    spot_copy().start()
    for step in range(blk_devs):
        chunk_copy(step).start()

    barrier = pltpu.get_barrier_semaphore()

    @pl.loop(1, n)
    def _(d):
        to = lax.rem(me + d, n)
        pl.semaphore_signal(
            barrier, inc=1, device_id=(lax.rem(to, freq_devs), to // freq_devs), device_id_type=MESH
        )

    row = lax.broadcasted_iota(jnp.int32, (cols, time_count), 0)
    time = lax.broadcasted_iota(jnp.int32, (cols, time_count), 1)
    period = freq_count * time_count
    low = band_ref[0]
    high = band_ref[1]
    numerator = low * freq_count + (high - low) * (row >> 1)
    turn = numerator * time

    def cosine(shift):
        return cos_turns(((turn + shift) & (period - 1)).astype(jnp.float32) * (1.0 / period))

    quarter = period // 4
    part = (row & 1) * quarter
    cos_full = cosine(part)
    sin_full = cosine(part + 3 * quarter)
    head = turn[:, :taps]
    lag = lax.broadcasted_iota(jnp.int32, (taps, taps), 0)
    late = lax.broadcasted_iota(jnp.int32, (taps, taps), 1)
    kept = jnp.where(lag < taps - late, 1.0, 0.0).astype(jnp.float32)
    fir = fir_ref[...]
    scale = 1.0 / math.sqrt(time_count)

    def head_cos(shift):
        return cos_turns(((head + shift) & (period - 1)).astype(jnp.float32) * (1.0 / period))

    sum_cos = dot(head_cos(0) * fir, kept, precision=lax.Precision.HIGHEST) * scale
    sum_sin = dot(head_cos(3 * quarter) * fir, kept, precision=lax.Precision.HIGHEST) * scale
    body = time_count - taps
    mixed = jnp.concatenate(
        [
            cos_full[:, :body] * sum_cos[:, :1] - sin_full[:, :body] * sum_sin[:, :1],
            cos_full[:, body:] * sum_cos - sin_full[:, body:] * sum_sin,
        ],
        1,
    )
    mixed_high = mixed.astype(jnp.bfloat16)
    table[pl.ds(0, cols), :] = mixed_high
    table[pl.ds(cols, cols), :] = (mixed - mixed_high.astype(jnp.float32)).astype(jnp.bfloat16)

    def spectrum_of(rows):
        both = dot(table[...], rows, NT_DIMS)
        return both[:cols] + both[cols:]

    spot_copy().wait()
    near = spectrum_of(spots_buf[...].reshape(spots * 16, time_count)).astype(jnp.bfloat16)
    spot_row = lax.broadcasted_iota(jnp.int32, (spots * 16, spot_lanes), 0)
    spot_col = lax.broadcasted_iota(jnp.int32, (spots * 16, spot_lanes), 1)
    pick = jnp.where(spot_row == spot_col * 16, 1.0, 0.0).astype(jnp.bfloat16)
    at_spots = dot(near, pick).reshape(freq_devs, PARTS, spot_lanes)
    at_spots = jnp.concatenate([at_spots, at_spots], 1).astype(jnp.bfloat16)
    pl.semaphore_wait(barrier, n - 1)

    def remote(step, f):
        block = lax.rem(me_b + step + 1, blk_devs)
        return pltpu.make_async_remote_copy(
            src_ref=outgoing.at[step, f],
            dst_ref=recv_ref.at[me],
            send_sem=send_sem.at[step * freq_devs + f],
            recv_sem=recv_sem.at[me],
            device_id=(f, block),
            device_id_type=MESH,
        )

    own = pltpu.make_async_copy(outgoing.at[blk_devs - 1, me_f], recv_ref.at[me], own_sem)
    for step in range(blk_devs):
        chunk_copy(step).wait()
        values = spectrum_of(
            traces_buf[pl.ds(step * per, per)].reshape(width, time_count)
        )
        values = values.reshape(freq_devs, PARTS, width)
        values = jnp.concatenate([values[:, :, :half], values[:, :, half:]], 1)
        outgoing[step, :, :, pl.ds(0, half)] = values.astype(jnp.bfloat16)
        outgoing[step, :, :, pl.ds(half, spot_lanes)] = at_spots
        first = 0
        if step == blk_devs - 1:
            own.start()
            first = 1

        @pl.loop(first, freq_devs)
        def _(d):
            remote(step, lax.rem(me_f + d, freq_devs)).start()

    own.wait()
    for step in range(blk_devs):

        @pl.loop(1 if step == blk_devs - 1 else 0, freq_devs)
        def _(d):
            remote(step, lax.rem(me_f + d, freq_devs)).wait_send()

    @pl.loop(1, n)
    def _(d):
        source = lax.rem(me + d, n)
        pltpu.make_async_remote_copy(
            src_ref=outgoing.at[0, 0],
            dst_ref=recv_ref.at[source],
            send_sem=send_sem.at[0],
            recv_sem=recv_sem.at[source],
            device_id=(lax.rem(source, freq_devs), source // freq_devs),
            device_id_type=MESH,
        ).wait_recv()


def product_kernel(targets_ref, recv_ref, out_ref):
    shots, rows, lanes = recv_ref.shape
    half = out_ref.shape[3] // 2
    spot_lanes = lanes - half
    depth = shots * rows
    count = targets_ref.shape[0]
    i = pl.program_id(0)
    received = recv_ref[...].reshape(depth, lanes)
    at_spots = received[:, half:]
    right = received[:, :half]
    column = lax.broadcasted_iota(jnp.int32, (count, depth), 1)
    base = targets_ref[...] * rows + 2 * i

    def chosen(part):
        return dot(jnp.where(column == base + part, 1.0, 0.0).astype(jnp.bfloat16), at_spots)

    real = chosen(0)
    imag = chosen(1)
    lefts = [
        jnp.concatenate([real, -imag], 1).astype(jnp.bfloat16),
        jnp.concatenate([imag, real], 1).astype(jnp.bfloat16),
    ]
    spot = lax.broadcasted_iota(jnp.int32, (2 * spot_lanes, depth), 0)
    place = lax.broadcasted_iota(jnp.int32, (2 * spot_lanes, depth), 1)
    home = jnp.where(spot < spot_lanes, spot * rows, (spot - spot_lanes) * rows + 1) + 2 * i
    scale = 1.0 / math.sqrt(shots)
    for h in range(2):
        spread = jnp.where(place == home + h * PARTS, 1.0, 0.0).astype(jnp.bfloat16)
        for o in range(2):
            left = dot(lefts[o], spread).astype(jnp.bfloat16)
            out_ref[0, o, :, pl.ds(h * half, half)] = dot(left, right) * scale


def per_device(traces, fir, targets, band):
    shot_dev, rec_count, time_count = traces.shape
    freq_devs = lax.axis_size("freq")
    blk_devs = lax.axis_size("blk")
    n = freq_devs * blk_devs
    assert shot_dev == 1
    col_stride = rec_count // n
    width = rec_count // blk_devs
    half = width // 2
    spot_lanes = max(128, n)
    lanes = half + spot_lanes
    cols = 2 * FREQ_DEV * freq_devs
    received = pl.pallas_call(
        functools.partial(send_kernel, freq_devs, blk_devs, col_stride),
        out_shape=jax.ShapeDtypeStruct((n, ROWS, lanes), jnp.bfloat16),
        in_specs=[
            pl.BlockSpec(memory_space=pltpu.SMEM),
            pl.BlockSpec(memory_space=pltpu.VMEM),
            pl.BlockSpec(memory_space=pl.ANY),
        ],
        out_specs=pl.BlockSpec(memory_space=pl.ANY),
        scratch_shapes=[
            pltpu.VMEM((n, col_stride, time_count), jnp.bfloat16),
            pltpu.VMEM((n, 16, time_count), jnp.bfloat16),
            pltpu.VMEM((2 * cols, time_count), jnp.bfloat16),
            pltpu.VMEM((blk_devs, freq_devs, ROWS, lanes), jnp.bfloat16),
            pltpu.SemaphoreType.DMA((blk_devs,)),
            pltpu.SemaphoreType.DMA,
            pltpu.SemaphoreType.DMA,
            pltpu.SemaphoreType.DMA((n,)),
            pltpu.SemaphoreType.DMA((n,)),
        ],
        compiler_params=pltpu.CompilerParams(
            collective_id=0, has_side_effects=True, vmem_limit_bytes=VMEM_LIMIT
        ),
    )(band, fir.reshape(1, -1), traces.reshape(n, col_stride, time_count))
    count = targets.shape[0]
    return pl.pallas_call(
        product_kernel,
        grid=(FREQ_DEV,),
        out_shape=jax.ShapeDtypeStruct((FREQ_DEV, 2, count, width), jnp.float32),
        in_specs=[
            pl.BlockSpec((count, 1), lambda i: (0, 0)),
            pl.BlockSpec((n, ROWS, lanes), lambda i: (0, 0, 0)),
        ],
        out_specs=pl.BlockSpec((1, 2, count, width), lambda i: (i, 0, 0, 0)),
        compiler_params=pltpu.CompilerParams(vmem_limit_bytes=VMEM_LIMIT),
    )(targets.reshape(-1, 1), received)


def solution(mesh):
    placed = (P(("blk", "freq"), None, None), P(), P(), P())
    return jax.shard_map(
        per_device,
        mesh=mesh,
        in_specs=placed,
        out_specs=P("freq", None, None, "blk"),
        check_vma=False,
    )
```

time: 192 us -> 34.2 us (0.18)
  the two profiles are of different devices: /device:TPU:0 before, /device:TPU:9 now
where the time goes in v1:
time: 34.2 us; the launch traced here: 34 us
  Pallas kernels  32.6 us (95%)
  local copies, waits for them, and re-layouts  1.45 us (4%)
    pallas_call x1, Pallas kernels, per_device(): pl.pallas_call(functools.partial(send_kernel, freq_devs, blk_devs, col_st...  23.7 us
    pallas_call x1, Pallas kernels, per_device(): pl.pallas_call(product_kernel, grid=(FREQ_DEV,), out_shape=jax.ShapeDtype...  8.83 us
    reshape x1, local copies, waits for them, and re-layouts, per_device(): targets.reshape(-1, 1)  1.45 us

profile of v1, /device:TPU:9, one launch (start us, length us, event | category | flops | bytes accessed | tf_op | source)
XLA Modules:
  0.0 34.0 jit_solution(2693470574977237602)
XLA Ops:
  0.0 1.5 %copy.5.targets_ref = s32[256,1]{1,0:T(8,128)} copy(s32[256,1]{0,1:T(1,128)} %bitcast.4) | data formatting | bytes 2048 | tf_op jit(solution)/shard_map/reshape | solution.py:260
  1.5 23.7 %shard_map.46.recv_ref = bf16[32,16,640]{2,1,0:T(8,128)(2,1)} custom-call(s32[2]{0:T(128)} %band_ref.1, f32[1,128]{1,0:T(1,128)} %bitcast.5, bf16[32,128,1024]{2,1,0:T(8,128)(2,1)} %bitcast.3), custom_call_target="tpu_custom_call" | custom-call | tf_op jit(solution)/shard_map/pallas_call | solution.py:225
  25.2 8.8 %shard_map.47 = f32[4,2,256,1024]{3,2,1,0:T(8,128)} custom-call(s32[256,1]{1,0:T(8,128)} %copy.5.targets_ref, bf16[32,16,640]{2,1,0:T(8,128)(2,1)} %shard_map.46.recv_ref), custom_call_target="tpu_custom_call" | custom-call | tf_op jit(solution)/shard_map/pallas_call | solution.py:250

commit v2 on v1

--- a/solution.py
+++ b/solution.py
@@ -28,6 +28,15 @@
         sign = 1.0 if order % 4 == 1 else -1.0
         total = total * w2 + sign / math.factorial(order)
     return -(total * w)
+
+
+def flipped(index, offset, count):
+    total = 0
+    bit = 1
+    while bit < count:
+        total = total + bit * lax.rem(index // bit + (offset // bit) % 2, 2)
+        bit *= 2
+    return total
 
 
 def send_kernel(
@@ -49,13 +58,16 @@
     per = width // col_stride
     spot_lanes = outgoing.shape[3] - half
 
+    crossing = list(range(blk_devs // 2, blk_devs))
+    offsets = crossing + list(range(blk_devs // 2 - 1, -1, -1))
+
     def spot_copy():
         return pltpu.make_async_copy(
             traces_ref.at[:, pl.ds(0, 16), :], spots_buf, spot_sem
         )
 
     def chunk_copy(step):
-        block = lax.rem(me_b + step + 1, blk_devs)
+        block = flipped(me_b, offsets[step], blk_devs)
         return pltpu.make_async_copy(
             traces_ref.at[pl.ds(block * per, per)],
             traces_buf.at[pl.ds(step * per, per)],
@@ -122,13 +134,14 @@
     near = spectrum_of(spots_buf[...].reshape(spots * 16, time_count)).astype(jnp.bfloat16)
     spot_row = lax.broadcasted_iota(jnp.int32, (spots * 16, spot_lanes), 0)
     spot_col = lax.broadcasted_iota(jnp.int32, (spots * 16, spot_lanes), 1)
-    pick = jnp.where(spot_row == spot_col * 16, 1.0, 0.0).astype(jnp.bfloat16)
+    spot_of = jnp.where(spot_col >= spots, spot_col - spots, spot_col)
+    pick = jnp.where(spot_row == spot_of * 16, 1.0, 0.0).astype(jnp.bfloat16)
     at_spots = dot(near, pick).reshape(freq_devs, PARTS, spot_lanes)
     at_spots = jnp.concatenate([at_spots, at_spots], 1).astype(jnp.bfloat16)
     pl.semaphore_wait(barrier, n - 1)
 
     def remote(step, f):
-        block = lax.rem(me_b + step + 1, blk_devs)
+        block = flipped(me_b, offsets[step], blk_devs)
         return pltpu.make_async_remote_copy(
             src_ref=outgoing.at[step, f],
             dst_ref=recv_ref.at[me],
@@ -180,34 +193,40 @@
 def product_kernel(targets_ref, recv_ref, out_ref):
     shots, rows, lanes = recv_ref.shape
     half = out_ref.shape[3] // 2
+    depth = shots * rows
     spot_lanes = lanes - half
-    depth = shots * rows
-    count = targets_ref.shape[0]
+    count = targets_ref.shape[1]
     i = pl.program_id(0)
-    received = recv_ref[...].reshape(depth, lanes)
-    at_spots = received[:, half:]
-    right = received[:, :half]
-    column = lax.broadcasted_iota(jnp.int32, (count, depth), 1)
-    base = targets_ref[...] * rows + 2 * i
-
-    def chosen(part):
-        return dot(jnp.where(column == base + part, 1.0, 0.0).astype(jnp.bfloat16), at_spots)
-
-    real = chosen(0)
-    imag = chosen(1)
-    lefts = [
-        jnp.concatenate([real, -imag], 1).astype(jnp.bfloat16),
-        jnp.concatenate([imag, real], 1).astype(jnp.bfloat16),
+
+    line = lax.broadcasted_iota(jnp.int32, (4 * shots, depth), 0)
+    place = lax.broadcasted_iota(jnp.int32, (4 * shots, depth), 1)
+    group = line // shots
+    home = (line - group * shots) * rows + (group // 2) * PARTS + (group & 1) + 2 * i
+    pick = jnp.where(place == home, 1.0, 0.0).astype(jnp.bfloat16)
+    picked = dot(pick, recv_ref[...].reshape(depth, lanes))
+
+    wanted = jnp.broadcast_to(targets_ref[...].astype(jnp.float32), (128, count)).T
+    shot = lax.broadcasted_iota(jnp.int32, (count, 2 * shots), 1)
+    shot = jnp.where(shot >= shots, shot - shots, shot)
+    chooser = jnp.where(shot == wanted[:, :1].astype(jnp.int32), 1.0, 0.0).astype(jnp.bfloat16)
+
+    near = picked[: 2 * shots, half:]
+    source = lax.broadcasted_iota(jnp.int32, near.shape, 0) >= shots
+    lane = lax.broadcasted_iota(jnp.int32, near.shape, 1)
+    target = lane >= shots
+    inside = lane < 2 * shots
+    same = inside & (source == target)
+    other = inside & (source != target)
+    parts = [
+        jnp.where(same, jnp.where(source, -near, near), 0.0),
+        jnp.where(other, near, 0.0),
     ]
-    spot = lax.broadcasted_iota(jnp.int32, (2 * spot_lanes, depth), 0)
-    place = lax.broadcasted_iota(jnp.int32, (2 * spot_lanes, depth), 1)
-    home = jnp.where(spot < spot_lanes, spot * rows, (spot - spot_lanes) * rows + 1) + 2 * i
+    lefts = [dot(chooser, p.astype(jnp.bfloat16)).astype(jnp.bfloat16) for p in parts]
     scale = 1.0 / math.sqrt(shots)
     for h in range(2):
-        spread = jnp.where(place == home + h * PARTS, 1.0, 0.0).astype(jnp.bfloat16)
+        right = picked[2 * shots * h : 2 * shots * (h + 1), :half].astype(jnp.bfloat16)
         for o in range(2):
-            left = dot(lefts[o], spread).astype(jnp.bfloat16)
-            out_ref[0, o, :, pl.ds(h * half, half)] = dot(left, right) * scale
+            out_ref[0, o, :, pl.ds(h * half, half)] = dot(lefts[o][:, : 2 * shots], right) * scale
 
 
 def per_device(traces, fir, targets, band):
@@ -216,10 +235,11 @@
     blk_devs = lax.axis_size("blk")
     n = freq_devs * blk_devs
     assert shot_dev == 1
+    assert blk_devs & (blk_devs - 1) == 0
     col_stride = rec_count // n
     width = rec_count // blk_devs
     half = width // 2
-    spot_lanes = max(128, n)
+    spot_lanes = max(128, 2 * n)
     lanes = half + spot_lanes
     cols = 2 * FREQ_DEV * freq_devs
     received = pl.pallas_call(
@@ -252,12 +272,12 @@
         grid=(FREQ_DEV,),
         out_shape=jax.ShapeDtypeStruct((FREQ_DEV, 2, count, width), jnp.float32),
         in_specs=[
-            pl.BlockSpec((count, 1), lambda i: (0, 0)),
+            pl.BlockSpec((1, count), lambda i: (0, 0)),
             pl.BlockSpec((n, ROWS, lanes), lambda i: (0, 0, 0)),
         ],
         out_specs=pl.BlockSpec((1, 2, count, width), lambda i: (i, 0, 0, 0)),
         compiler_params=pltpu.CompilerParams(vmem_limit_bytes=VMEM_LIMIT),
-    )(targets.reshape(-1, 1), received)
+    )(targets.reshape(1, -1), received)
 
 
 def solution(mesh):

time: 34.2 us -> 29.4 us (0.86)
  the two profiles are of different devices: /device:TPU:9 before, /device:TPU:0 now
where the time goes in v2:
time: 29.4 us; the launch traced here: 28.9 us
  Pallas kernels  28.9 us (98%)
    pallas_call x1, Pallas kernels, per_device(): pl.pallas_call(functools.partial(send_kernel, freq_devs, blk_devs, col_st...  22.7 us
    pallas_call x1, Pallas kernels, per_device(): pl.pallas_call(product_kernel, grid=(FREQ_DEV,), out_shape=jax.ShapeDtype...  6.15 us

profile of v2, /device:TPU:0, one launch (start us, length us, event | category | flops | bytes accessed | tf_op | source)
XLA Modules:
  0.0 28.9 jit_solution(1256410037912048309)
XLA Ops:
  0.0 22.7 %shard_map.46.recv_ref = bf16[32,16,640]{2,1,0:T(8,128)(2,1)} custom-call(s32[2]{0:T(128)} %band_ref.1, f32[1,128]{1,0:T(1,128)} %bitcast.5, bf16[32,128,1024]{2,1,0:T(8,128)(2,1)} %bitcast.3), custom_call_target="tpu_custom_call" | custom-call | tf_op jit(solution)/shard_map/pallas_call | solution.py:245
  22.7 6.2 %shard_map.47 = f32[4,2,256,1024]{3,2,1,0:T(8,128)} custom-call(s32[1,256]{1,0:T(1,128)} %bitcast.4, bf16[32,16,640]{2,1,0:T(8,128)(2,1)} %shard_map.46.recv_ref), custom_call_target="tpu_custom_call" | custom-call | tf_op jit(solution)/shard_map/pallas_call | solution.py:270

commit v3 on v2

--- a/solution.py
+++ b/solution.py
@@ -41,8 +41,10 @@
 
 def send_kernel(
     freq_devs, blk_devs, col_stride,
-    band_ref, fir_ref, traces_ref, recv_ref,
-    traces_buf, spots_buf, table, outgoing, chunk_sem, spot_sem, own_sem, send_sem, recv_sem,
+    band_ref, fir_ref, traces_ref, recv_ref, plane_ref,
+    traces_buf, spots_buf, table, outgoing, near_out, near_in, plane_out,
+    chunk_sem, spot_sem, own_sem, send_sem, recv_sem,
+    near_send, near_recv, plane_own, plane_send, plane_recv,
 ):
     me_f = lax.axis_index("freq")
     me_b = lax.axis_index("blk")
@@ -56,7 +58,8 @@
     cols = 2 * freq_count
     taps = fir_ref.shape[1]
     per = width // col_stride
-    spot_lanes = outgoing.shape[3] - half
+    _, near_rows, near_lanes = near_out.shape
+    packed = near_lanes // spots
 
     crossing = list(range(blk_devs // 2, blk_devs))
     offsets = crossing + list(range(blk_devs // 2 - 1, -1, -1))
@@ -132,13 +135,41 @@
 
     spot_copy().wait()
     near = spectrum_of(spots_buf[...].reshape(spots * 16, time_count)).astype(jnp.bfloat16)
-    spot_row = lax.broadcasted_iota(jnp.int32, (spots * 16, spot_lanes), 0)
-    spot_col = lax.broadcasted_iota(jnp.int32, (spots * 16, spot_lanes), 1)
-    spot_of = jnp.where(spot_col >= spots, spot_col - spots, spot_col)
-    pick = jnp.where(spot_row == spot_of * 16, 1.0, 0.0).astype(jnp.bfloat16)
-    at_spots = dot(near, pick).reshape(freq_devs, PARTS, spot_lanes)
-    at_spots = jnp.concatenate([at_spots, at_spots], 1).astype(jnp.bfloat16)
+    spot_row = lax.broadcasted_iota(jnp.int32, (spots * 16, near_lanes), 0)
+    spot_col = lax.broadcasted_iota(jnp.int32, (spots * 16, near_lanes), 1)
+    shift = lax.rem(me_f, packed) * spots
+    pick = jnp.where(spot_row == (spot_col - shift) * 16, 1.0, 0.0).astype(jnp.bfloat16)
+    at_spots = dot(near, pick).reshape(freq_devs, PARTS, near_lanes)
+    at_spots = jnp.concatenate([at_spots] * (near_rows // PARTS), 1)
+    line = lax.broadcasted_iota(jnp.int32, at_spots.shape, 1) // PARTS
+    near_out[...] = jnp.where(line == me_f // packed, at_spots, 0.0).astype(jnp.bfloat16)
     pl.semaphore_wait(barrier, n - 1)
+
+    def near_copy(f, slot):
+        return pltpu.make_async_remote_copy(
+            src_ref=near_out.at[f],
+            dst_ref=near_in.at[slot],
+            send_sem=near_send.at[f],
+            recv_sem=near_recv.at[slot],
+            device_id=(f, me_b),
+            device_id_type=MESH,
+        )
+
+    def plane_copy(offset, slot):
+        return pltpu.make_async_remote_copy(
+            src_ref=plane_out,
+            dst_ref=plane_ref.at[slot],
+            send_sem=plane_send.at[offset],
+            recv_sem=plane_recv.at[slot],
+            device_id=(me_f, flipped(me_b, offset, blk_devs)),
+            device_id_type=MESH,
+        )
+
+    own_plane = pltpu.make_async_copy(plane_out, plane_ref.at[me_b], plane_own)
+
+    @pl.loop(1, freq_devs)
+    def _(d):
+        near_copy(lax.rem(me_f + d, freq_devs), me_f).start()
 
     def remote(step, f):
         block = flipped(me_b, offsets[step], blk_devs)
@@ -159,8 +190,7 @@
         )
         values = values.reshape(freq_devs, PARTS, width)
         values = jnp.concatenate([values[:, :, :half], values[:, :, half:]], 1)
-        outgoing[step, :, :, pl.ds(0, half)] = values.astype(jnp.bfloat16)
-        outgoing[step, :, :, pl.ds(half, spot_lanes)] = at_spots
+        outgoing[step] = values.astype(jnp.bfloat16)
         first = 0
         if step == blk_devs - 1:
             own.start()
@@ -170,7 +200,27 @@
         def _(d):
             remote(step, lax.rem(me_f + d, freq_devs)).start()
 
+        if step == blk_devs // 2 - 1:
+            total = near_out[me_f].astype(jnp.float32)
+            for d in range(1, freq_devs):
+                source = lax.rem(me_f + d, freq_devs)
+                near_copy(source, source).wait_recv()
+                total = total + near_in[source].astype(jnp.float32)
+            plane_out[...] = total.astype(jnp.bfloat16)
+            own_plane.start()
+            for offset in range(1, blk_devs):
+                plane_copy(offset, me_b).start()
+
     own.wait()
+    own_plane.wait()
+
+    @pl.loop(1, freq_devs)
+    def _(d):
+        near_copy(lax.rem(me_f + d, freq_devs), me_f).wait_send()
+
+    for offset in range(1, blk_devs):
+        plane_copy(offset, me_b).wait_send()
+        plane_copy(offset, flipped(me_b, offset, blk_devs)).wait_recv()
     for step in range(blk_devs):
 
         @pl.loop(1 if step == blk_devs - 1 else 0, freq_devs)
@@ -190,11 +240,12 @@
         ).wait_recv()
 
 
-def product_kernel(targets_ref, recv_ref, out_ref):
+def product_kernel(freq_devs, targets_ref, recv_ref, plane_ref, out_ref):
     shots, rows, lanes = recv_ref.shape
+    blk_devs, near_rows, near_lanes = plane_ref.shape
+    packed = near_lanes // shots
     half = out_ref.shape[3] // 2
     depth = shots * rows
-    spot_lanes = lanes - half
     count = targets_ref.shape[1]
     i = pl.program_id(0)
 
@@ -210,7 +261,22 @@
     shot = jnp.where(shot >= shots, shot - shots, shot)
     chooser = jnp.where(shot == wanted[:, :1].astype(jnp.int32), 1.0, 0.0).astype(jnp.bfloat16)
 
-    near = picked[: 2 * shots, half:]
+    near_depth = blk_devs * near_rows
+    line = lax.broadcasted_iota(jnp.int32, (2 * shots, near_depth), 0)
+    place = lax.broadcasted_iota(jnp.int32, (2 * shots, near_depth), 1)
+    part = line // shots
+    from_shot = line - part * shots
+    from_f = from_shot % freq_devs
+    home = (from_shot // freq_devs) * near_rows + (from_f // packed) * PARTS + 2 * i + part
+    pick = jnp.where(place == home, 1.0, 0.0).astype(jnp.bfloat16)
+    near = dot(pick, plane_ref[...].reshape(near_depth, near_lanes))
+    slot = lax.broadcasted_iota(jnp.int32, near.shape, 0) % freq_devs % packed
+    lane = lax.broadcasted_iota(jnp.int32, near.shape, 1)
+    near = jnp.where(lane // shots == slot, near, 0.0).astype(jnp.bfloat16)
+    fold_row = lax.broadcasted_iota(jnp.int32, (near_lanes, max(128, 2 * shots)), 0)
+    fold_col = lax.broadcasted_iota(jnp.int32, (near_lanes, max(128, 2 * shots)), 1)
+    fold = jnp.where(fold_row % shots == fold_col % shots, 1.0, 0.0).astype(jnp.bfloat16)
+    near = dot(near, fold)
     source = lax.broadcasted_iota(jnp.int32, near.shape, 0) >= shots
     lane = lax.broadcasted_iota(jnp.int32, near.shape, 1)
     target = lane >= shots
@@ -239,28 +305,41 @@
     col_stride = rec_count // n
     width = rec_count // blk_devs
     half = width // 2
-    spot_lanes = max(128, 2 * n)
-    lanes = half + spot_lanes
+    lanes = half
+    near_lanes = max(128, n)
+    packed = near_lanes // n
+    near_rows = freq_devs // packed * PARTS
     cols = 2 * FREQ_DEV * freq_devs
-    received = pl.pallas_call(
+    received, planes = pl.pallas_call(
         functools.partial(send_kernel, freq_devs, blk_devs, col_stride),
-        out_shape=jax.ShapeDtypeStruct((n, ROWS, lanes), jnp.bfloat16),
+        out_shape=[
+            jax.ShapeDtypeStruct((n, ROWS, lanes), jnp.bfloat16),
+            jax.ShapeDtypeStruct((blk_devs, near_rows, near_lanes), jnp.bfloat16),
+        ],
         in_specs=[
             pl.BlockSpec(memory_space=pltpu.SMEM),
             pl.BlockSpec(memory_space=pltpu.VMEM),
             pl.BlockSpec(memory_space=pl.ANY),
         ],
-        out_specs=pl.BlockSpec(memory_space=pl.ANY),
+        out_specs=[pl.BlockSpec(memory_space=pl.ANY)] * 2,
         scratch_shapes=[
             pltpu.VMEM((n, col_stride, time_count), jnp.bfloat16),
             pltpu.VMEM((n, 16, time_count), jnp.bfloat16),
             pltpu.VMEM((2 * cols, time_count), jnp.bfloat16),
             pltpu.VMEM((blk_devs, freq_devs, ROWS, lanes), jnp.bfloat16),
+            pltpu.VMEM((freq_devs, near_rows, near_lanes), jnp.bfloat16),
+            pltpu.VMEM((freq_devs, near_rows, near_lanes), jnp.bfloat16),
+            pltpu.VMEM((near_rows, near_lanes), jnp.bfloat16),
             pltpu.SemaphoreType.DMA((blk_devs,)),
             pltpu.SemaphoreType.DMA,
             pltpu.SemaphoreType.DMA,
             pltpu.SemaphoreType.DMA((n,)),
             pltpu.SemaphoreType.DMA((n,)),
+            pltpu.SemaphoreType.DMA((freq_devs,)),
+            pltpu.SemaphoreType.DMA((freq_devs,)),
+            pltpu.SemaphoreType.DMA,
+            pltpu.SemaphoreType.DMA((blk_devs,)),
+            pltpu.SemaphoreType.DMA((blk_devs,)),
         ],
         compiler_params=pltpu.CompilerParams(
             collective_id=0, has_side_effects=True, vmem_limit_bytes=VMEM_LIMIT
@@ -268,16 +347,17 @@
     )(band, fir.reshape(1, -1), traces.reshape(n, col_stride, time_count))
     count = targets.shape[0]
     return pl.pallas_call(
-        product_kernel,
+        functools.partial(product_kernel, freq_devs),
         grid=(FREQ_DEV,),
         out_shape=jax.ShapeDtypeStruct((FREQ_DEV, 2, count, width), jnp.float32),
         in_specs=[
             pl.BlockSpec((1, count), lambda i: (0, 0)),
             pl.BlockSpec((n, ROWS, lanes), lambda i: (0, 0, 0)),
+            pl.BlockSpec((blk_devs, near_rows, near_lanes), lambda i: (0, 0, 0)),
         ],
         out_specs=pl.BlockSpec((1, 2, count, width), lambda i: (i, 0, 0, 0)),
         compiler_params=pltpu.CompilerParams(vmem_limit_bytes=VMEM_LIMIT),
-    )(targets.reshape(1, -1), received)
+    )(targets.reshape(1, -1), received, planes)
 
 
 def solution(mesh):

time: 29.4 us -> 30.2 us (1.027); the launches traced: 28.9 us -> 30 us
  Pallas kernels: 28.9 us -> 30 us
    pallas_call x1, Pallas kernels: 22.7 us -> 23.6 us  [per_device(): pl.pallas_call(functools.partial(send_kernel, freq_devs, blk_devs, col_st...]
where the time goes in v3:
time: 30.2 us; the launch traced here: 30 us
  Pallas kernels  30 us (99%)
    pallas_call x1, Pallas kernels, per_device(): pl.pallas_call(functools.partial(send_kernel, freq_devs, blk_devs, col_st...  23.6 us
    pallas_call x1, Pallas kernels, per_device(): pl.pallas_call(functools.partial(product_kernel, freq_devs), grid=(FREQ_D...  6.43 us

profile of v3, /device:TPU:0, one launch (start us, length us, event | category | flops | bytes accessed | tf_op | source)
XLA Modules:
  0.0 30.0 jit_solution(2128835738511706576)
XLA Ops:
  0.0 23.6 %shard_map.46 = (bf16[32,16,512]{2,1,0:T(8,128)(2,1)}, bf16[4,16,128]{2,1,0:T(8,128)(2,1)}) custom-call(s32[2]{0:T(128)} %band_ref.1, f32[1,128]{1,0:T(1,128)} %bitcast.5, bf16[32,128,1024]{2,1,0:T(8,128)(2,1)} %bitcast.3), custom_call_target="tpu_custom_call" | custom-call | tf_op jit(solution)/shard_map/pallas_call | solution.py:313
  23.6 6.4 %shard_map.47 = f32[4,2,256,1024]{3,2,1,0:T(8,128)} custom-call(s32[1,256]{1,0:T(1,128)} %bitcast.4, bf16[32,16,512]{2,1,0:T(8,128)(2,1)} %get-tuple-element.7.recv_ref, bf16[4,16,128]{2,1,0:T(8,128)(2,1)} %get-tuple-element.8.plane_ref), custom_call_target="tpu_custom_call" | custom-call | tf_op jit(solution)/shard_map/pallas_call | solution.py:349

commit v4 on v3

--- a/solution.py
+++ b/solution.py
@@ -77,8 +77,9 @@
             chunk_sem.at[step],
         )
 
+    chunk_copy(0).start()
     spot_copy().start()
-    for step in range(blk_devs):
+    for step in range(1, blk_devs):
         chunk_copy(step).start()
 
     barrier = pltpu.get_barrier_semaphore()
@@ -133,16 +134,6 @@
         both = dot(table[...], rows, NT_DIMS)
         return both[:cols] + both[cols:]
 
-    spot_copy().wait()
-    near = spectrum_of(spots_buf[...].reshape(spots * 16, time_count)).astype(jnp.bfloat16)
-    spot_row = lax.broadcasted_iota(jnp.int32, (spots * 16, near_lanes), 0)
-    spot_col = lax.broadcasted_iota(jnp.int32, (spots * 16, near_lanes), 1)
-    shift = lax.rem(me_f, packed) * spots
-    pick = jnp.where(spot_row == (spot_col - shift) * 16, 1.0, 0.0).astype(jnp.bfloat16)
-    at_spots = dot(near, pick).reshape(freq_devs, PARTS, near_lanes)
-    at_spots = jnp.concatenate([at_spots] * (near_rows // PARTS), 1)
-    line = lax.broadcasted_iota(jnp.int32, at_spots.shape, 1) // PARTS
-    near_out[...] = jnp.where(line == me_f // packed, at_spots, 0.0).astype(jnp.bfloat16)
     pl.semaphore_wait(barrier, n - 1)
 
     def near_copy(f, slot):
@@ -166,10 +157,6 @@
         )
 
     own_plane = pltpu.make_async_copy(plane_out, plane_ref.at[me_b], plane_own)
-
-    @pl.loop(1, freq_devs)
-    def _(d):
-        near_copy(lax.rem(me_f + d, freq_devs), me_f).start()
 
     def remote(step, f):
         block = flipped(me_b, offsets[step], blk_devs)
@@ -200,7 +187,23 @@
         def _(d):
             remote(step, lax.rem(me_f + d, freq_devs)).start()
 
-        if step == blk_devs // 2 - 1:
+        if step == 0:
+            spot_copy().wait()
+            near = spectrum_of(spots_buf[...].reshape(spots * 16, time_count)).astype(jnp.bfloat16)
+            spot_row = lax.broadcasted_iota(jnp.int32, (spots * 16, near_lanes), 0)
+            spot_col = lax.broadcasted_iota(jnp.int32, (spots * 16, near_lanes), 1)
+            shift = lax.rem(me_f, packed) * spots
+            pick = jnp.where(spot_row == (spot_col - shift) * 16, 1.0, 0.0).astype(jnp.bfloat16)
+            at_spots = dot(near, pick).reshape(freq_devs, PARTS, near_lanes)
+            at_spots = jnp.concatenate([at_spots] * (near_rows // PARTS), 1)
+            line = lax.broadcasted_iota(jnp.int32, at_spots.shape, 1) // PARTS
+            near_out[...] = jnp.where(line == me_f // packed, at_spots, 0.0).astype(jnp.bfloat16)
+
+            @pl.loop(1, freq_devs)
+            def _(d):
+                near_copy(lax.rem(me_f + d, freq_devs), me_f).start()
+
+        if step == blk_devs - 2:
             total = near_out[me_f].astype(jnp.float32)
             for d in range(1, freq_devs):
                 source = lax.rem(me_f + d, freq_devs)
@@ -240,59 +243,69 @@
         ).wait_recv()
 
 
-def product_kernel(freq_devs, targets_ref, recv_ref, plane_ref, out_ref):
+def product_kernel(freq_devs, targets_ref, recv_ref, plane_ref, out_ref, made, sems):
     shots, rows, lanes = recv_ref.shape
     blk_devs, near_rows, near_lanes = plane_ref.shape
     packed = near_lanes // shots
-    half = out_ref.shape[3] // 2
+    half = made.shape[3] // 2
     depth = shots * rows
     count = targets_ref.shape[1]
-    i = pl.program_id(0)
-
-    line = lax.broadcasted_iota(jnp.int32, (4 * shots, depth), 0)
-    place = lax.broadcasted_iota(jnp.int32, (4 * shots, depth), 1)
-    group = line // shots
-    home = (line - group * shots) * rows + (group // 2) * PARTS + (group & 1) + 2 * i
-    pick = jnp.where(place == home, 1.0, 0.0).astype(jnp.bfloat16)
-    picked = dot(pick, recv_ref[...].reshape(depth, lanes))
 
     wanted = jnp.broadcast_to(targets_ref[...].astype(jnp.float32), (128, count)).T
     shot = lax.broadcasted_iota(jnp.int32, (count, 2 * shots), 1)
     shot = jnp.where(shot >= shots, shot - shots, shot)
     chooser = jnp.where(shot == wanted[:, :1].astype(jnp.int32), 1.0, 0.0).astype(jnp.bfloat16)
-
-    near_depth = blk_devs * near_rows
-    line = lax.broadcasted_iota(jnp.int32, (2 * shots, near_depth), 0)
-    place = lax.broadcasted_iota(jnp.int32, (2 * shots, near_depth), 1)
-    part = line // shots
-    from_shot = line - part * shots
-    from_f = from_shot % freq_devs
-    home = (from_shot // freq_devs) * near_rows + (from_f // packed) * PARTS + 2 * i + part
-    pick = jnp.where(place == home, 1.0, 0.0).astype(jnp.bfloat16)
-    near = dot(pick, plane_ref[...].reshape(near_depth, near_lanes))
-    slot = lax.broadcasted_iota(jnp.int32, near.shape, 0) % freq_devs % packed
-    lane = lax.broadcasted_iota(jnp.int32, near.shape, 1)
-    near = jnp.where(lane // shots == slot, near, 0.0).astype(jnp.bfloat16)
     fold_row = lax.broadcasted_iota(jnp.int32, (near_lanes, max(128, 2 * shots)), 0)
     fold_col = lax.broadcasted_iota(jnp.int32, (near_lanes, max(128, 2 * shots)), 1)
     fold = jnp.where(fold_row % shots == fold_col % shots, 1.0, 0.0).astype(jnp.bfloat16)
-    near = dot(near, fold)
-    source = lax.broadcasted_iota(jnp.int32, near.shape, 0) >= shots
-    lane = lax.broadcasted_iota(jnp.int32, near.shape, 1)
-    target = lane >= shots
-    inside = lane < 2 * shots
-    same = inside & (source == target)
-    other = inside & (source != target)
-    parts = [
-        jnp.where(same, jnp.where(source, -near, near), 0.0),
-        jnp.where(other, near, 0.0),
-    ]
-    lefts = [dot(chooser, p.astype(jnp.bfloat16)).astype(jnp.bfloat16) for p in parts]
     scale = 1.0 / math.sqrt(shots)
-    for h in range(2):
-        right = picked[2 * shots * h : 2 * shots * (h + 1), :half].astype(jnp.bfloat16)
+
+    def write(i, o):
+        return pltpu.make_async_copy(made.at[i, o], out_ref.at[i, o], sems.at[i, o])
+
+    for i in range(FREQ_DEV):
+        line = lax.broadcasted_iota(jnp.int32, (4 * shots, depth), 0)
+        place = lax.broadcasted_iota(jnp.int32, (4 * shots, depth), 1)
+        group = line // shots
+        home = (line - group * shots) * rows + (group // 2) * PARTS + (group & 1) + 2 * i
+        pick = jnp.where(place == home, 1.0, 0.0).astype(jnp.bfloat16)
+        picked = dot(pick, recv_ref[...].reshape(depth, lanes))
+
+        near_depth = blk_devs * near_rows
+        line = lax.broadcasted_iota(jnp.int32, (2 * shots, near_depth), 0)
+        place = lax.broadcasted_iota(jnp.int32, (2 * shots, near_depth), 1)
+        part = line // shots
+        from_shot = line - part * shots
+        from_f = from_shot % freq_devs
+        home = (from_shot // freq_devs) * near_rows + (from_f // packed) * PARTS + 2 * i + part
+        pick = jnp.where(place == home, 1.0, 0.0).astype(jnp.bfloat16)
+        near = dot(pick, plane_ref[...].reshape(near_depth, near_lanes))
+        slot = lax.broadcasted_iota(jnp.int32, near.shape, 0) % freq_devs % packed
+        lane = lax.broadcasted_iota(jnp.int32, near.shape, 1)
+        near = jnp.where(lane // shots == slot, near, 0.0).astype(jnp.bfloat16)
+        near = dot(near, fold)
+        source = lax.broadcasted_iota(jnp.int32, near.shape, 0) >= shots
+        lane = lax.broadcasted_iota(jnp.int32, near.shape, 1)
+        target = lane >= shots
+        inside = lane < 2 * shots
+        same = inside & (source == target)
+        other = inside & (source != target)
+        parts = [
+            jnp.where(same, jnp.where(source, -near, near), 0.0),
+            jnp.where(other, near, 0.0),
+        ]
+        lefts = [dot(chooser, p.astype(jnp.bfloat16)).astype(jnp.bfloat16) for p in parts]
+        rights = [
+            picked[2 * shots * h : 2 * shots * (h + 1), :half].astype(jnp.bfloat16) for h in range(2)
+        ]
         for o in range(2):
-            out_ref[0, o, :, pl.ds(h * half, half)] = dot(lefts[o][:, : 2 * shots], right) * scale
+            for h in range(2):
+                made[i, o, :, pl.ds(h * half, half)] = dot(lefts[o][:, : 2 * shots], rights[h]) * scale
+            write(i, o).start()
+
+    for i in range(FREQ_DEV):
+        for o in range(2):
+            write(i, o).wait()
 
 
 def per_device(traces, fir, targets, band):
@@ -348,14 +361,13 @@
     count = targets.shape[0]
     return pl.pallas_call(
         functools.partial(product_kernel, freq_devs),
-        grid=(FREQ_DEV,),
         out_shape=jax.ShapeDtypeStruct((FREQ_DEV, 2, count, width), jnp.float32),
-        in_specs=[
-            pl.BlockSpec((1, count), lambda i: (0, 0)),
-            pl.BlockSpec((n, ROWS, lanes), lambda i: (0, 0, 0)),
-            pl.BlockSpec((blk_devs, near_rows, near_lanes), lambda i: (0, 0, 0)),
-        ],
-        out_specs=pl.BlockSpec((1, 2, count, width), lambda i: (i, 0, 0, 0)),
+        in_specs=[pl.BlockSpec(memory_space=pltpu.VMEM)] * 3,
+        out_specs=pl.BlockSpec(memory_space=pl.ANY),
+        scratch_shapes=[
+            pltpu.VMEM((FREQ_DEV, 2, count, width), jnp.float32),
+            pltpu.SemaphoreType.DMA((FREQ_DEV, 2)),
+        ],
         compiler_params=pltpu.CompilerParams(vmem_limit_bytes=VMEM_LIMIT),
     )(targets.reshape(1, -1), received, planes)
 

time: 30.2 us -> 29 us (0.960)
  Pallas kernels: 30 us -> 28.9 us
    pallas_call x1, Pallas kernels: 6.43 us -> 5.31 us  [per_device(): pl.pallas_call(functools.partial(product_kernel, freq_devs), out_shape=ja...]
where the time goes in v4:
time: 29 us; the launch traced here: 28.9 us
  Pallas kernels  28.9 us (100%)
    pallas_call x1, Pallas kernels, per_device(): pl.pallas_call(functools.partial(send_kernel, freq_devs, blk_devs, col_st...  23.6 us
    pallas_call x1, Pallas kernels, per_device(): pl.pallas_call(functools.partial(product_kernel, freq_devs), out_shape=ja...  5.31 us

profile of v4, /device:TPU:0, one launch (start us, length us, event | category | flops | bytes accessed | tf_op | source)
XLA Modules:
  0.0 28.9 jit_solution(1505739487097062102)
XLA Ops:
  0.0 23.6 %shard_map.46 = (bf16[32,16,512]{2,1,0:T(8,128)(2,1)}, bf16[4,16,128]{2,1,0:T(8,128)(2,1)}) custom-call(s32[2]{0:T(128)} %band_ref.1, f32[1,128]{1,0:T(1,128)} %bitcast.5, bf16[32,128,1024]{2,1,0:T(8,128)(2,1)} %bitcast.3), custom_call_target="tpu_custom_call" | custom-call | tf_op jit(solution)/shard_map/pallas_call | solution.py:326
  23.6 5.3 %shard_map.47 = f32[4,2,256,1024]{3,2,1,0:T(8,128)} custom-call(s32[1,256]{1,0:T(1,128)} %bitcast.4, bf16[32,16,512]{2,1,0:T(8,128)(2,1)} %get-tuple-element.7.recv_ref, bf16[4,16,128]{2,1,0:T(8,128)(2,1)} %get-tuple-element.8.plane_ref), custom_call_target="tpu_custom_call" | custom-call | tf_op jit(solution)/shard_map/pallas_call | solution.py:362

commit v5 on v4

--- a/solution.py
+++ b/solution.py
@@ -134,7 +134,6 @@
         both = dot(table[...], rows, NT_DIMS)
         return both[:cols] + both[cols:]
 
-    pl.semaphore_wait(barrier, n - 1)
 
     def near_copy(f, slot):
         return pltpu.make_async_remote_copy(
@@ -178,6 +177,8 @@
         values = values.reshape(freq_devs, PARTS, width)
         values = jnp.concatenate([values[:, :, :half], values[:, :, half:]], 1)
         outgoing[step] = values.astype(jnp.bfloat16)
+        if step == 0:
+            pl.semaphore_wait(barrier, n - 1)
         first = 0
         if step == blk_devs - 1:
             own.start()

time: 29 us -> 28.2 us (0.972)
  Pallas kernels: 28.9 us -> 28 us
    pallas_call x1, Pallas kernels: 23.6 us -> 22.7 us  [per_device(): pl.pallas_call(functools.partial(send_kernel, freq_devs, blk_devs, col_st...]
where the time goes in v5:
time: 28.2 us; the launch traced here: 28.1 us
  Pallas kernels  28 us (99%)
    pallas_call x1, Pallas kernels, per_device(): pl.pallas_call(functools.partial(send_kernel, freq_devs, blk_devs, col_st...  22.7 us
    pallas_call x1, Pallas kernels, per_device(): pl.pallas_call(functools.partial(product_kernel, freq_devs), out_shape=ja...  5.32 us

profile of v5, /device:TPU:0, one launch (start us, length us, event | category | flops | bytes accessed | tf_op | source)
XLA Modules:
  0.0 28.1 jit_solution(3654900518022179994)
XLA Ops:
  0.0 22.7 %shard_map.46 = (bf16[32,16,512]{2,1,0:T(8,128)(2,1)}, bf16[4,16,128]{2,1,0:T(8,128)(2,1)}) custom-call(s32[2]{0:T(128)} %band_ref.1, f32[1,128]{1,0:T(1,128)} %bitcast.5, bf16[32,128,1024]{2,1,0:T(8,128)(2,1)} %bitcast.3), custom_call_target="tpu_custom_call" | custom-call | tf_op jit(solution)/shard_map/pallas_call | solution.py:327
  22.7 5.3 %shard_map.47 = f32[4,2,256,1024]{3,2,1,0:T(8,128)} custom-call(s32[1,256]{1,0:T(1,128)} %bitcast.4, bf16[32,16,512]{2,1,0:T(8,128)(2,1)} %get-tuple-element.7.recv_ref, bf16[4,16,128]{2,1,0:T(8,128)(2,1)} %get-tuple-element.8.plane_ref), custom_call_target="tpu_custom_call" | custom-call | tf_op jit(solution)/shard_map/pallas_call | solution.py:363

commit v6 on v5

--- a/solution.py
+++ b/solution.py
@@ -13,7 +13,6 @@
 ROWS = 2 * PARTS
 VMEM_LIMIT = 56 * 2**20
 MESH = pl.DeviceIdType.MESH
-NT_DIMS = (((1,), (1,)), ((), ()))
 
 
 def dot(a, b, dims=(((1,), (0,)), ((), ())), precision=None):
@@ -127,11 +126,13 @@
         1,
     )
     mixed_high = mixed.astype(jnp.bfloat16)
-    table[pl.ds(0, cols), :] = mixed_high
-    table[pl.ds(cols, cols), :] = (mixed - mixed_high.astype(jnp.float32)).astype(jnp.bfloat16)
+    mixed_low = mixed - mixed_high.astype(jnp.float32)
+    table[...] = (
+        jnp.concatenate([mixed_high.astype(jnp.float32), mixed_low], 0).T.astype(jnp.bfloat16)
+    )
 
     def spectrum_of(rows):
-        both = dot(table[...], rows, NT_DIMS)
+        both = dot(rows, table[...]).T
         return both[:cols] + both[cols:]
 
 
@@ -339,7 +340,7 @@
         scratch_shapes=[
             pltpu.VMEM((n, col_stride, time_count), jnp.bfloat16),
             pltpu.VMEM((n, 16, time_count), jnp.bfloat16),
-            pltpu.VMEM((2 * cols, time_count), jnp.bfloat16),
+            pltpu.VMEM((time_count, 2 * cols), jnp.bfloat16),
             pltpu.VMEM((blk_devs, freq_devs, ROWS, lanes), jnp.bfloat16),
             pltpu.VMEM((freq_devs, near_rows, near_lanes), jnp.bfloat16),
             pltpu.VMEM((freq_devs, near_rows, near_lanes), jnp.bfloat16),

time: 28.2 us -> 28.2 us (level)
  no operation moved by 1% of the time
where the time goes in v6:
time: 28.2 us; the launch traced here: 28 us
  Pallas kernels  28 us (99%)
    pallas_call x1, Pallas kernels, per_device(): pl.pallas_call(functools.partial(send_kernel, freq_devs, blk_devs, col_st...  22.7 us
    pallas_call x1, Pallas kernels, per_device(): pl.pallas_call(functools.partial(product_kernel, freq_devs), out_shape=ja...  5.3 us

profile of v6, /device:TPU:0, one launch (start us, length us, event | category | flops | bytes accessed | tf_op | source)
XLA Modules:
  0.0 28.0 jit_solution(1613278847005954008)
XLA Ops:
  0.0 22.7 %shard_map.46 = (bf16[32,16,512]{2,1,0:T(8,128)(2,1)}, bf16[4,16,128]{2,1,0:T(8,128)(2,1)}) custom-call(s32[2]{0:T(128)} %band_ref.1, f32[1,128]{1,0:T(1,128)} %bitcast.5, bf16[32,128,1024]{2,1,0:T(8,128)(2,1)} %bitcast.3), custom_call_target="tpu_custom_call" | custom-call | tf_op jit(solution)/shard_map/pallas_call | solution.py:328
  22.7 5.3 %shard_map.47 = f32[4,2,256,1024]{3,2,1,0:T(8,128)} custom-call(s32[1,256]{1,0:T(1,128)} %bitcast.4, bf16[32,16,512]{2,1,0:T(8,128)(2,1)} %get-tuple-element.7.recv_ref, bf16[4,16,128]{2,1,0:T(8,128)(2,1)} %get-tuple-element.8.plane_ref), custom_call_target="tpu_custom_call" | custom-call | tf_op jit(solution)/shard_map/pallas_call | solution.py:364
